TPU v7x, 256 devices: a whole 4x4x8 slice. The times are simulated.
256 devices in a mesh: lat: 64 (over x_hi, y, z), lev: 4 (over x_lo, core).
Axes of the slice: x: 4 (x_hi: 2, x_lo: 2; x = x_hi * 2 + x_lo), y: 4, z: 8, core: 2. Of those that a mesh axis runs over, the one named last changes fastest.
Arguments:
- tracers: float32 [9, 16, 1474560], P(None, 'lev', 'lat'), may hold values from 0 to 1
- delp: float32 [16, 1474560], P('lev', 'lat'), may hold values from 0.8 to 1.2
- theta: float32 [16, 1474560], P('lev', 'lat'), may hold values from 0.8 to 1.2
- wind_x: float32 [16, 1474560], P('lev', 'lat'), may hold values from -0.04 to 0.04
- wind_y: float32 [16, 1474560], P('lev', 'lat'), may hold values from -0.04 to 0.04
- surface: float32 [1474560], P('lat'), may hold values from -6 to 6
- level_weight: float32 [16], replicated, may hold values from 0.5 to 2
Outputs:
- new_tracers: float32 [9, 16, 1474560], P(None, 'lev', 'lat')
- new_theta: float32 [16, 1474560], P('lev', 'lat')
- new_delp: float32 [16, 1474560], P('lev', 'lat')
- geopotential: float32 [16, 1474560], P('lev', 'lat')
All inputs are finite; a program needn't handle non-finite values.
Results may differ from a plain program's by a relative error of at most 0.000023.
Values sent between devices are 32-bit elements; how exact they have to be, the bound alone decides.
No kernel may reach another device: no remote copies, remote signals or barrier semaphores. Data moves between devices by JAX's collectives and lax.ppermute only.
A program may use at most 256 MiB of HBM per device.

v0:
```python
import functools

import jax
import jax.numpy as jnp
from jax import lax
from jax.experimental import pallas as pl
from jax.experimental.pallas import tpu as pltpu
from jax.sharding import PartitionSpec as P

NLON = 2880
WIDE = 2944
HALF = 4
ROWS = 8
LAYERS = 4
BLOCK = 3840
TOP = 1.0
ROW_UNROLL = 4
SMOOTH_UNROLL = 4
PAIR_UNROLL = 2
SPLIT = 4
VMEM_LIMIT = 60 * 1024 * 1024


def params(**extra):
    return pltpu.CompilerParams(vmem_limit_bytes=VMEM_LIMIT, **extra)


SMALL = pl.CostEstimate(flops=1000, bytes_accessed=1000, transcendentals=0)


def shift(x, by):
    return pltpu.roll(x, by % WIDE, 1)


def wrap(x, odd):
    if odd:
        x = shift(x, -64)
    lane = lax.broadcasted_iota(jnp.int32, (8, 128), 1)
    first, last = x[:, :128], x[:, WIDE - 128 :]
    ends = jnp.where(lane < 96, pltpu.roll(first, 64, 1), pltpu.roll(last, 64, 1))
    last = jnp.where(lane < 64, last, ends)
    return jnp.concatenate([x[:, : WIDE - 128], last], axis=1)


def widen(own, north, south, put):
    def pairs(source, count, first):
        def pair(i, carry):
            base = pl.multiple_of(i * (2 * NLON), 128)
            put(first + 2 * i, wrap(source(base), False))
            put(first + 2 * i + 1, wrap(source(base + NLON - 64), True))
            return carry

        lax.fori_loop(0, count, pair, 0, unroll=PAIR_UNROLL)

    pairs(north, HALF // 2, 0)
    pairs(own, ROWS // 2, HALF)
    pairs(south, HALF // 2, HALF + ROWS)


def advance(f_ref, a_ref, b_ref, c_ref, out_ref, count, offset):
    def face(i):
        return a_ref[i + offset] * (
            7.0 * (f_ref[i + 1] + f_ref[i + 2]) - (f_ref[i] + f_ref[i + 3])
        )

    def row(i, carry):
        f = f_ref[i + 2]
        west, east = shift(f, 1), shift(f, -1)
        west_flux = b_ref[i + offset] * (7.0 * (west + f) - (shift(f, 2) + east))
        east_flux = c_ref[i + offset] * (7.0 * (f + east) - (west + shift(f, -2)))
        out_ref[i] = f - (face(i + 1) - face(i)) - (east_flux - west_flux)
        return carry

    lax.fori_loop(0, count, row, 0, unroll=ROW_UNROLL)


def smooth(f_ref, k_ref):
    def row(i, carry):
        k = k_ref[i]
        keep = 1.0 - 2.0 * k
        f = f_ref[i]
        near = shift(f, 1) + shift(f, -1)
        middle = shift(f, 2) + shift(f, -2)
        outer = shift(f, 3) + shift(f, -3)
        f_ref[i] = (
            (keep * keep * keep + 6.0 * keep * k * k) * f
            + (3.0 * keep * keep * k + 3.0 * k * k * k) * near
            + (3.0 * keep * k * k) * middle
            + (k * k * k) * outer
        )
        return carry

    largest = k_ref[0]
    for i in range(1, ROWS):
        largest = jnp.maximum(largest, k_ref[i])

    @pl.when(largest > 0.0)
    def _():
        lax.fori_loop(0, ROWS, row, 0, unroll=SMOOTH_UNROLL)


def emit(f_ref, store, scale_ref=None):
    lane = lax.broadcasted_iota(jnp.int32, (8, 128), 1)

    def pair(i, carry):
        even, odd = f_ref[2 * i], f_ref[2 * i + 1]
        if scale_ref is not None:
            even, odd = even * scale_ref[2 * i], odd * scale_ref[2 * i + 1]
        odd = shift(odd, 64)
        middle = jnp.where(lane < 64, even[:, WIDE - 128 :], odd[:, :128])
        base = pl.multiple_of(i * (2 * NLON), 128)
        store(base, jnp.concatenate([even[:, : WIDE - 128], middle, odd[:, 128:]], axis=1))
        return carry

    lax.fori_loop(0, ROWS // 2, pair, 0, unroll=PAIR_UNROLL)


def both(x):
    return jnp.concatenate([x, x], axis=0)


def prepare_kernel(
    lat_total, row_ref, k_ref, delp_ref, wx_ref, wy_ref, north_ref, south_ref,
    thick_ref, a_ref, b_ref, c_ref, d_ref, r_ref, x_ref, f1_ref, f2_ref,
):
    def load(ref, field, put):
        widen(
            lambda at: both(ref[:, pl.ds(at, WIDE)]),
            lambda at: both(north_ref[field, :, pl.ds(at, WIDE)]),
            lambda at: both(south_ref[field, :, pl.ds(at, WIDE)]),
            put,
        )

    first = row_ref[0]

    def put_x(r, x):
        x_ref[r] = x

    def put_d(r, x):
        d_ref[r] = x

    load(wy_ref, 2, put_x)

    def face(i, carry):
        at = first + (i - 2)
        scale = jnp.where((at > 0) & (at < lat_total), 1.0 / 24.0, 0.0)
        a_ref[i] = scale * (x_ref[i + 1] + x_ref[i + 2])
        return carry

    lax.fori_loop(0, 13, face, 0)
    load(wx_ref, 1, put_x)

    def east(i, carry):
        w = x_ref[i + 2]
        b_ref[i] = (1.0 / 24.0) * (shift(w, 1) + w)
        c_ref[i] = (1.0 / 24.0) * (w + shift(w, -1))
        return carry

    lax.fori_loop(0, 12, east, 0, unroll=2)
    load(delp_ref, 0, put_d)
    advance(d_ref, a_ref, b_ref, c_ref, f1_ref, 12, 0)
    advance(f1_ref, a_ref, b_ref, c_ref, f2_ref, 8, 2)
    smooth(f2_ref, k_ref)

    def store(base, x):
        thick_ref[:, pl.ds(base, x.shape[1])] = x[:LAYERS]

    emit(f2_ref, store)

    def invert(i, carry):
        r_ref[i] = 1.0 / f2_ref[i]
        return carry

    lax.fori_loop(0, ROWS, invert, 0)


def whole(*shape):
    return pl.BlockSpec(shape, lambda *_: (0,) * len(shape))


def prepare(first_row, k, delp, wx, wy, north, south, lat_total):
    rows = (13, 12, 12, 16, 8)
    flat = whole(*delp.shape)
    halo = whole(*north.shape)
    smem = pl.BlockSpec(memory_space=pltpu.SMEM)
    return pl.pallas_call(
        functools.partial(prepare_kernel, lat_total),
        grid=(1,),
        out_shape=[jax.ShapeDtypeStruct(delp.shape, jnp.float32)]
        + [jax.ShapeDtypeStruct((n, 8, WIDE), jnp.float32) for n in rows],
        in_specs=[smem, smem, flat, flat, flat, halo, halo],
        out_specs=[flat] + [whole(n, 8, WIDE) for n in rows],
        scratch_shapes=[
            pltpu.VMEM((n, 8, WIDE), jnp.float32) for n in (16, 12, 8)
        ],
        compiler_params=params(),
        cost_estimate=SMALL,
        name="prepare",
    )(first_row, k, delp, wx, wy, north, south)


def transport_kernel(with_theta, *refs):
    if with_theta:
        theta_ref, *refs = refs
    (
        k_ref, lower_ref, upper_ref, north_ref, south_ref,
        a_ref, b_ref, c_ref, d_ref, r_ref, first_ref, last_ref, f0_ref, f1_ref, f2_ref,
    ) = refs
    pair = pl.program_id(0)

    def lower(s):
        x = lower_ref[0, :, pl.ds(s, WIDE)]
        if not with_theta:
            return x
        return jnp.where(pair == 0, theta_ref[:, pl.ds(s, WIDE)], x)

    def put(r, x):
        f0_ref[r] = x * d_ref[r]

    widen(
        lambda at: jnp.concatenate([lower(at), upper_ref[0, :, pl.ds(at, WIDE)]], axis=0),
        lambda at: jnp.concatenate(
            [north_ref[0, :, pl.ds(at, WIDE)], north_ref[1, :, pl.ds(at, WIDE)]], axis=0
        ),
        lambda at: jnp.concatenate(
            [south_ref[0, :, pl.ds(at, WIDE)], south_ref[1, :, pl.ds(at, WIDE)]], axis=0
        ),
        put,
    )
    advance(f0_ref, a_ref, b_ref, c_ref, f1_ref, 12, 0)
    advance(f1_ref, a_ref, b_ref, c_ref, f2_ref, 8, 2)
    smooth(f2_ref, k_ref)

    def store(base, x):
        at = pl.ds(base, x.shape[1])
        for field in range(2):
            first_ref[field, :, at] = x[LAYERS * field : LAYERS * field + 2]
            last_ref[field, :, at] = x[LAYERS * field + 2 : LAYERS * field + 4]

    emit(f2_ref, store, r_ref)


def transport(pairs, first, theta, k, tracers, north, south, *rows):
    cells = tracers.shape[2]
    lead = 0 if theta is None else 1
    field = lambda index: pl.BlockSpec((1, LAYERS, cells), index)
    halo = pl.BlockSpec((2, LAYERS, HALF * NLON), lambda p: (p, 0, 0))
    in_specs = [
        pl.BlockSpec(memory_space=pltpu.SMEM),
        field(lambda p: (jnp.maximum(first + 2 * p - lead, first), 0, 0)),
        field(lambda p: (first + 2 * p + 1 - lead, 0, 0)),
        halo, halo, *[whole(*x.shape) for x in rows],
    ]
    args = [k, tracers, tracers, north, south, *rows]
    half = pl.BlockSpec((2, 2, cells), lambda p: (p, 0, 0))
    if lead:
        in_specs = [whole(*theta.shape)] + in_specs
        args = [theta] + args
    return pl.pallas_call(
        functools.partial(transport_kernel, bool(lead)),
        grid=(pairs,),
        out_shape=[jax.ShapeDtypeStruct((2 * pairs, 2, cells), jnp.float32)] * 2,
        in_specs=in_specs,
        out_specs=[half, half],
        scratch_shapes=[
            pltpu.VMEM((n, 8, WIDE), jnp.float32) for n in (16, 12, 8)
        ],
        compiler_params=params(),
        cost_estimate=SMALL,
        name="transport",
    )(*args)


def edges_kernel(
    rows, weight_ref, lev_ref, thick_ref,
    ov_ref, delp_ref, log_ref, choice_ref, edge_ref, flag_ref,
):
    wrapped, places = rows
    groups, _, width = thick_ref.shape
    levels = groups * LAYERS
    lev = lev_ref[0]
    sums = [jnp.float32(0.0)]
    for l in range(levels):
        sums.append(sums[-1] + weight_ref[l])
    edge = jnp.full((1, width), TOP, jnp.float32)
    marks = []
    for l in range(levels):
        edge_ref[l // LAYERS, l % LAYERS : l % LAYERS + 1] = edge
        marks.append(edge)
        edge = edge + thick_ref[l // LAYERS, l % LAYERS : l % LAYERS + 1]
    scale = (edge - TOP) / jnp.full((1, width), sums[levels], jnp.float32)
    level = lax.broadcasted_iota(jnp.int32, (LAYERS, width), 0)
    low = jnp.zeros((LAYERS, width), jnp.float32)
    high = low
    own = [sums[i] for i in range(LAYERS + 1)]
    for g in range(1, groups):
        own = [jnp.where(lev == g, sums[g * LAYERS + i], own[i]) for i in range(LAYERS + 1)]
    for i in range(LAYERS):
        low = jnp.where(level == i, own[i], low)
        high = jnp.where(level == i, own[i + 1], high)
    low, high = TOP + low * scale, TOP + high * scale
    delp = high - low
    delp_ref[...] = delp
    log_ref[...] = jnp.log(high / low)
    inverse = 1.0 / delp
    for i, (away, l) in enumerate(places):
        if wrapped:
            group = lax.rem(lev + away + groups, groups)
        else:
            group = jnp.clip(lev + away, 0, groups - 1)
        base = jnp.broadcast_to(edge_ref[group, l : l + 1], (LAYERS, width))
        limit = jnp.broadcast_to(thick_ref[group, l : l + 1], (LAYERS, width))
        part = jnp.minimum(jnp.maximum(high - base, 0.0), limit) - jnp.minimum(
            jnp.maximum(low - base, 0.0), limit
        )
        ov_ref[i] = part * inverse

    step = pl.program_id(0)

    @pl.when(step == 0)
    def _():
        flag_ref[...] = jnp.full(flag_ref.shape, -1.0, jnp.float32)

    worst = [None, None]
    for m in range(LAYERS, levels, LAYERS):
        target = TOP + sums[m] * scale
        for i in range(2):
            over = jnp.maximum(marks[m - 2 - i] - target, target - marks[m + 2 + i])
            worst[i] = over if worst[i] is None else jnp.maximum(worst[i], over)
    for i in range(2):
        best = worst[i][:, :128]
        for c in range(128, width, 128):
            best = jnp.maximum(best, worst[i][:, c : c + 128])
        flag_ref[i : i + 1] = jnp.maximum(flag_ref[i : i + 1], best)

    @pl.when(step == pl.num_programs(0) - 1)
    def _():
        two, three = jnp.max(flag_ref[0:1]), jnp.max(flag_ref[1:2])
        choice_ref[0] = jnp.where(two <= 0.0, 0, jnp.where(three <= 0.0, 1, 2))


def edges(weight, lev, thick, rows):
    groups, _, cells = thick.shape
    count = len(rows[1])
    smem = pl.BlockSpec(memory_space=pltpu.SMEM)
    own = pl.BlockSpec((LAYERS, BLOCK), lambda i: (0, i))
    level = jax.ShapeDtypeStruct((LAYERS, cells), jnp.float32)
    return pl.pallas_call(
        functools.partial(edges_kernel, rows),
        grid=(cells // BLOCK,),
        out_shape=[
            jax.ShapeDtypeStruct((count, LAYERS, cells), jnp.float32),
            level, level, jax.ShapeDtypeStruct((1,), jnp.int32),
        ],
        in_specs=[smem, smem, pl.BlockSpec((groups, LAYERS, BLOCK), lambda i: (0, 0, i))],
        out_specs=[
            pl.BlockSpec((count, LAYERS, BLOCK), lambda i: (0, 0, i)),
            own, own, smem,
        ],
        scratch_shapes=[
            pltpu.VMEM((groups, LAYERS, BLOCK), jnp.float32),
            pltpu.VMEM((8, 128), jnp.float32),
        ],
        compiler_params=params(),
        cost_estimate=SMALL,
        name="edges",
    )(weight, lev, thick)


def mix(sources, firsts, ov_ref, field):
    width = ov_ref.shape[2]
    total = None
    for density, first in zip(sources, firsts):
        for l in range(density.shape[1]):
            x = jnp.broadcast_to(density[field, l : l + 1], (LAYERS, width))
            term = x * ov_ref[first + l]
            total = term if total is None else total + term
    return total


def theta_kernel(firsts, *refs):
    n = len(firsts)
    ov_ref, log_ref, surface_ref, theta_ref, part_ref, sum_ref = refs[n:]
    theta = mix(refs[:n], firsts, ov_ref, 0)
    theta_ref[...] = theta
    column = theta * log_ref[...]
    partial = jnp.zeros((1, column.shape[1]), jnp.float32)
    for k in range(LAYERS - 1, -1, -1):
        partial = partial + column[k : k + 1]
        part_ref[k : k + 1] = partial + surface_ref[...]
    sum_ref[...] = partial


def tracer_kernel(firsts, *refs):
    n = len(firsts)
    one, two, ov_ref, out_ref = refs[:n], refs[n : 2 * n], refs[-2], refs[-1]
    for q in range(SPLIT):
        out_ref[q] = mix(two, firsts, ov_ref, q)
    for q in range(SPLIT, out_ref.shape[0]):
        out_ref[q] = mix(one, firsts, ov_ref, q - SPLIT + 1)


def flat_spec(shape, count=None):
    lead = tuple(shape[:-1]) if count is None else (count,) + tuple(shape[1:-1])
    return pl.BlockSpec(lead + (BLOCK,), lambda i: (0,) * len(lead) + (i,))


def columnwise(kernel, args, specs, outs, name):
    cells = outs[0][-1]
    return pl.pallas_call(
        kernel,
        grid=(cells // BLOCK,),
        out_shape=[jax.ShapeDtypeStruct(o, jnp.float32) for o in outs],
        in_specs=specs,
        out_specs=[flat_spec(o) for o in outs],
        compiler_params=params(),
        cost_estimate=SMALL,
        name=name,
    )(*args)


def remap_theta(sources, firsts, overlap, log_ratio, surface):
    cells = surface.shape[1]
    args = [*sources, overlap, log_ratio, surface]
    specs = [flat_spec(x.shape, 1) for x in sources]
    specs += [flat_spec(overlap.shape, used(sources)), flat_spec(log_ratio.shape)]
    specs += [flat_spec(surface.shape)]
    level = (LAYERS, cells)
    return columnwise(
        functools.partial(theta_kernel, firsts), args, specs,
        [level, level, (1, cells)], "remap_theta",
    )


def used(sources):
    return sum(x.shape[1] for x in sources)


def remap_tracers(one, two, firsts, overlap, tracers):
    args = [*one, *two]
    specs = [flat_spec(x.shape) for x in args]
    specs += [flat_spec(overlap.shape, used(one))]
    return columnwise(
        functools.partial(tracer_kernel, firsts), [*args, overlap], specs,
        [(tracers, LAYERS, overlap.shape[2])], "remap_tracers",
    )[0]


def on_device(lat_total, tracers, delp, theta, wind_x, wind_y, surface, level_weight):
    count, layers, cells = tracers.shape
    bands, groups = lax.axis_size("lat"), lax.axis_size("lev")
    band, lev = lax.axis_index("lat"), lax.axis_index("lev")
    half = HALF * NLON
    to_south = [(i, i + 1) for i in range(bands - 1)]
    to_north = [(i + 1, i) for i in range(bands - 1)]

    def beside(parts):
        last = jnp.concatenate([p[:, :, half:] for p in parts], axis=0)
        leading = jnp.concatenate([p[:, :, :half] for p in parts], axis=0)
        return lax.ppermute(last, "lat", to_south), lax.ppermute(leading, "lat", to_north)

    first_row = (band * ROWS).astype(jnp.int32)
    row_index = (first_row + jnp.arange(ROWS, dtype=jnp.int32)).astype(jnp.float32)
    latitude = jnp.pi * ((row_index + 0.5) / lat_total - 0.5)
    k = 0.25 * jnp.maximum(0.0, 1.0 - 2.0 * jnp.cos(latitude))
    north, south = beside([delp[None], wind_x[None], wind_y[None]])
    halo_one = beside([theta[None], tracers[SPLIT:]])
    halo_two = beside([tracers[:SPLIT]])
    thick, *rows = prepare(
        first_row[None], k, delp, wind_x, wind_y, north, south, lat_total
    )
    thick_all = lax.all_gather(thick, "lev", axis=0)
    down = lambda by: [(i + by, i) for i in range(groups - by)]
    up = lambda by: [(i, i + by) for i in range(groups - by)]

    def window(first, last):
        return lax.ppermute(last, "lev", up(1)), lax.ppermute(first, "lev", down(1))

    one = transport((count - SPLIT + 1) // 2, SPLIT, theta, k, tracers, *halo_one, *rows)
    near_one = window(*one)
    two = transport(SPLIT // 2, 0, None, k, tracers, *halo_two, *rows)
    near_two = window(*two)
    places = [(0, l) for l in range(LAYERS)]
    places += [(-1, 2), (-1, 3), (1, 0), (1, 1), (-1, 1), (1, 2)]
    overlap, new_delp, log_ratio, choice = edges(
        level_weight, lev[None], thick_all, (False, places)
    )

    def finish(one, two, firsts, overlap, log_ratio, surface):
        new_theta, partial, total = remap_theta(one, firsts, overlap, log_ratio, surface)
        above = sum(lax.ppermute(total, "lev", down(by)) for by in range(1, groups))
        new_tracers = remap_tracers(one, two, firsts, overlap, count)
        return new_tracers, new_theta, partial + above

    def reach_two(one, two, overlap, log_ratio, surface, thick_all):
        return finish(one, two, (0, 2, 4, 6), overlap, log_ratio, surface)

    def reach_three(one, two, overlap, log_ratio, surface, thick_all):
        def more(first, last, *near):
            return (first, last, *near, *window(last[:, :1], first[:, 1:]))

        firsts = (0, 2, 4, 6, 8, 9)
        return finish(more(*one), more(*two), firsts, overlap, log_ratio, surface)

    def reach_all(one, two, overlap, log_ratio, surface, thick_all):
        places = [(-by, l) for by in range(groups) for l in range(LAYERS)]
        overlap = edges(level_weight, lev[None], thick_all, (True, places))[0]

        def around(x):
            turned = [
                lax.ppermute(x, "lev", [(i, (i + by) % groups) for i in range(groups)])
                for by in range(1, groups)
            ]
            return [x, *turned]

        def spread(first, last, *near):
            return (*around(first), *around(last))

        starts = range(0, groups * LAYERS, LAYERS)
        firsts = (*starts, *(i + 2 for i in starts))
        return finish(spread(*one), spread(*two), firsts, overlap, log_ratio, surface)

    new_tracers, new_theta, geopotential = lax.switch(
        choice[0],
        [reach_two, reach_three, reach_all],
        (*one, *near_one), (*two, *near_two), overlap, log_ratio, surface[None], thick_all,
    )
    return new_tracers, new_theta, new_delp, geopotential


def solution(mesh):
    lat_total = ROWS * mesh.shape["lat"]
    return jax.shard_map(
        functools.partial(on_device, lat_total),
        mesh=mesh,
        in_specs=(
            P(None, "lev", "lat"),
            P("lev", "lat"),
            P("lev", "lat"),
            P("lev", "lat"),
            P("lev", "lat"),
            P("lat"),
            P(),
        ),
        out_specs=(P(None, "lev", "lat"), P("lev", "lat"), P("lev", "lat"), P("lev", "lat")),
        check_vma=False,
    )
```

profile of v0, /device:TPU:99, one launch (start us, length us, event | category | flops | bytes accessed | tf_op | source)
XLA Modules:
  0.0 142.8 jit_solution(1464101582614866742)
XLA Ops:
  8.3 1.4 fusion.3
  10.6 4.7 %collective-permute-start.25 = (f32[3,4,11520]{2,1,0:T(4,128)}, f32[3,4,11520]{2,1,0:T(4,128)}, u32[]{:S(2)}, u32[]{:S(2)}) collective-permute-start(f32[3,4,11520]{2,1,0:T(4,128)} %pad_maximum_fusion.2), channel_id=1, source_target_pairs={{0,4},{4,8},{8,12},{12,16},{16,20},{20,24},{24,28},{28,32},{32,36}... | collective-permute-start | bytes 1658888 | tf_op jit(solution)/shard_map/ppermute | solution.py:460
  16.3 1.9 %collective-permute-start.26 = (f32[3,4,11520]{2,1,0:T(4,128)}, f32[3,4,11520]{2,1,0:T(4,128)}, u32[]{:S(2)}, u32[]{:S(2)}) collective-permute-start(f32[3,4,11520]{2,1,0:T(4,128)} %pad_maximum_fusion.3), channel_id=1, source_target_pairs={{4,0},{8,4},{12,8},{16,12},{20,16},{24,20},{28,24},{32,28},{36,32}... | collective-permute-start | bytes 1658888 | tf_op jit(solution)/shard_map/ppermute | solution.py:460
  18.4 1.3 pad_maximum_fusion
  19.7 4.6 %collective-permute-start.27 = (f32[6,4,11520]{2,1,0:T(4,128)}, f32[6,4,11520]{2,1,0:T(4,128)}, u32[]{:S(2)}, u32[]{:S(2)}) collective-permute-start(f32[6,4,11520]{2,1,0:T(4,128)} %pad_maximum_fusion), channel_id=1, source_target_pairs={{0,4},{4,8},{8,12},{12,16},{16,20},{20,24},{24,28},{28,32},{32,36}... | collective-permute-start | bytes 3317768 | tf_op jit(solution)/shard_map/ppermute | solution.py:460
  25.5 1.9 %collective-permute-start.28 = (f32[6,4,11520]{2,1,0:T(4,128)}, f32[6,4,11520]{2,1,0:T(4,128)}, u32[]{:S(2)}, u32[]{:S(2)}) collective-permute-start(f32[6,4,11520]{2,1,0:T(4,128)} %pad_maximum_fusion.1), channel_id=1, source_target_pairs={{4,0},{8,4},{12,8},{16,12},{20,16},{24,20},{28,24},{32,28},{36,32}... | collective-permute-start | bytes 3317768 | tf_op jit(solution)/shard_map/ppermute | solution.py:460
  28.0 4.8 %collective-permute-done.26.south_ref = f32[3,4,11520]{2,1,0:T(4,128)} collective-permute-done((f32[3,4,11520]{2,1,0:T(4,128)}, f32[3,4,11520]{2,1,0:T(4,128)}, u32[]{:S(2)}, u32[]{:S(2)}) %collective-permute-start.26) | collective-permute-done | bytes 552992 | tf_op jit(solution)/shard_map/ppermute | solution.py:460
  32.8 11.7 %prepare.1 = (f32[4,23040]{1,0:T(4,128)}, f32[13,8,2944]{2,1,0:T(8,128)}, f32[12,8,2944]{2,1,0:T(8,128)}, f32[12,8,2944]{2,1,0:T(8,128)}, f32[16,8,2944]{2,1,0:T(8,128)}, /*index=5*/f32[8,8,2944]{2,1,0:T(8,128)}) custom-call(s32[1]{0:T(128)} %bitcast.2.row_ref, f32[8]{0:T(128)} %maximum_multiply_fusion.k_ref.refs_1_.refs_0_, f32[4,23040]{1,0:T(4,128)} %delp_ref.1, ...), custom_call_target="tpu_custom_call" | custom-call | flops 1000 | bytes 1000 | tf_op jit(solution)/shard_map/prepare/pallas_call | solution.py:186
  45.7 1.9 %collective-permute-start.32 = (f32[4,4,11520]{2,1,0:T(4,128)}, f32[4,4,11520]{2,1,0:T(4,128)S(1)}, u32[]{:S(2)}, u32[]{:S(2)}) collective-permute-start(f32[4,4,11520]{2,1,0:T(4,128)} %get-tuple-element.141), channel_id=1, source_target_pairs={{4,0},{8,4},{12,8},{16,12},{20,16},{24,20},{28,24},{32,28},{36,32}... | collective-permute-start | bytes 2211848 | tf_op jit(solution)/shard_map/ppermute | solution.py:460
  47.6 4.6 %collective-permute-start.31 = (f32[4,4,11520]{2,1,0:T(4,128)}, f32[4,4,11520]{2,1,0:T(4,128)S(1)}, u32[]{:S(2)}, u32[]{:S(2)}) collective-permute-start(f32[4,4,11520]{2,1,0:T(4,128)} %get-tuple-element.142), channel_id=1, source_target_pairs={{0,4},{4,8},{8,12},{12,16},{16,20},{20,24},{24,28},{28,32},{32,36}... | collective-permute-start | bytes 2211848 | tf_op jit(solution)/shard_map/ppermute | solution.py:460
  52.2 4.3 %collective-permute-done.28.refs_5_ = f32[6,4,11520]{2,1,0:T(4,128)} collective-permute-done((f32[6,4,11520]{2,1,0:T(4,128)}, f32[6,4,11520]{2,1,0:T(4,128)}, u32[]{:S(2)}, u32[]{:S(2)}) %collective-permute-start.28) | collective-permute-done | bytes 1105952 | tf_op jit(solution)/shard_map/ppermute | solution.py:460
  56.5 19.4 %transport.2 = (f32[6,2,23040]{2,1,0:T(2,128)}, f32[6,2,23040]{2,1,0:T(2,128)}) custom-call(f32[4,23040]{1,0:T(4,128)} %refs_0_.1, f32[8]{0:T(128)} %maximum_multiply_fusion.k_ref.refs_1_.refs_0_, f32[9,4,23040]{2,1,0:T(4,128)} %refs_2_.3, f32[9,4,23040]{2,1,0:T(4,128)} %refs_2_.3, f32[6,4,11520]{2,1,0:T(4,128)} %collective-permute-done.27.refs_4_, ...), custom_call_target="tpu_custom_call" | custom-call | flops 1000 | bytes 1000 | tf_op jit(solution)/shard_map/transport/pallas_call | solution.py:259
  75.9 6.0 %collective-permute-start.30 = (f32[6,2,23040]{2,1,0:T(2,128)}, f32[6,2,23040]{2,1,0:T(2,128)}, u32[]{:S(2)}, u32[]{:S(2)}) collective-permute-start(f32[6,2,23040]{2,1,0:T(2,128)} %get-tuple-element.131), channel_id=1, source_target_pairs={{1,0},{2,1},{3,2},{5,4},{6,5},{7,6},{9,8},{10,9},{11,10},{13,12},{... | collective-permute-start | bytes 3317768 | tf_op jit(solution)/shard_map/ppermute | solution.py:477
  81.9 1.4 collective-permute-start.29
  85.2 13.7 %transport.3 = (f32[4,2,23040]{2,1,0:T(2,128)}, f32[4,2,23040]{2,1,0:T(2,128)}) custom-call(f32[8]{0:T(128)} %maximum_multiply_fusion.k_ref.refs_1_.refs_0_, f32[9,4,23040]{2,1,0:T(4,128)} %refs_2_.3, f32[9,4,23040]{2,1,0:T(4,128)} %refs_2_.3, f32[4,4,11520]{2,1,0:T(4,128)} %copy-done.7, f32[4,4,11520]{2,1,0:T(4,128)} %copy-done.6, ...), custom_call_target="tpu_custom_call" | custom-call | flops 1000 | bytes 1000 | tf_op jit(solution)/shard_map/transport/pallas_call | solution.py:259
  98.8 3.9 %collective-permute-start.34 = (f32[4,2,23040]{2,1,0:T(2,128)}, f32[4,2,23040]{2,1,0:T(2,128)}, u32[]{:S(2)}, u32[]{:S(2)}) collective-permute-start(f32[4,2,23040]{2,1,0:T(2,128)} %get-tuple-element.133), channel_id=1, source_target_pairs={{1,0},{2,1},{3,2},{5,4},{6,5},{7,6},{9,8},{10,9},{11,10},{13,12},{... | collective-permute-start | bytes 2211848 | tf_op jit(solution)/shard_map/ppermute | solution.py:477
  102.8 1.3 collective-permute-start.33
  104.8 6.9 %edges.3 = (f32[10,4,23040]{2,1,0:T(4,128)S(1)}, f32[4,23040]{1,0:T(4,128)}, f32[4,23040]{1,0:T(4,128)S(1)}, s32[1]{0:T(128)}) custom-call(f32[16]{0:T(128)S(1)} %copy-done.14, s32[1]{0:T(128)} %bitcast.1.lev_ref, f32[4,4,23040]{2,1,0:T(4,128)} %all-gather.4.cloned.1.call-done.thick_ref), custom_call_target="tpu_custom_call" | custom-call | flops 1000 | bytes 1000 | tf_op jit(solution)/shard_map/edges/pallas_call | solution.py:348
  112.3 22.8 %conditional.1 = (f32[9,4,23040]{2,1,0:T(4,128)}, f32[4,23040]{1,0:T(4,128)}, f32[4,23040]{1,0:T(4,128)S(1)}) conditional(s32[]{:T(128)} %bitcast.7, (f32[6,2,23040]{2,1,0:T(2,128)}, f32[6,2,23040]{2,1,0:T(2,128)}, f32[6,2,23040]{2,1,0:T(2,128)}, f32[6,2,23040]{2,1,0:T(2,128)}, f32[4,2,23040]{2,1,0:T(2,128)}, ...), branch_computations={%region_0.0_spmd, %region_1.0_spmd, %region_2.0_spmd} | conditional | flops 141240 | bytes 64607952 | solution.py:523
  112.3 4.3 %remap_theta.3 = (f32[4,23040]{1,0:T(4,128)}, f32[4,23040]{1,0:T(4,128)}, f32[1,23040]{1,0:T(1,128)}) custom-call(f32[6,2,23040]{2,1,0:T(2,128)} %get-tuple-element.62.refs_0_, f32[6,2,23040]{2,1,0:T(2,128)} %get-tuple-element.63.refs_1_, f32[6,2,23040]{2,1,0:T(2,128)} %get-tuple-element.64.refs_2_, f32[6,2,23040]{2,1,0:T(2,128)} %get-tuple-element.65.refs_3_, ...), custom_call_target="tpu_custom_call" | custom-call | flops 1000 | bytes 1000 | tf_op jit(solution)/shard_map/cond/branch_0_fun/remap_theta/pallas_call | solution.py:410
  116.6 3.7 %collective-permute-start.2 = (f32[1,23040]{1,0:T(1,128)}, f32[1,23040]{1,0:T(1,128)}, u32[]{:S(2)}, u32[]{:S(2)}) collective-permute-start(f32[1,23040]{1,0:T(1,128)} %get-tuple-element.75), channel_id=1, source_target_pairs={{3,0},{7,4},{11,8},{15,12},{19,16},{23,20},{27,24},{31,28},{35,32}... | collective-permute-start | bytes 276488 | tf_op jit(solution)/shard_map/cond/branch_0_fun/ppermute | solution.py:491
  120.3 1.9 %collective-permute-start.1 = (f32[1,23040]{1,0:T(1,128)}, f32[1,23040]{1,0:T(1,128)}, u32[]{:S(2)}, u32[]{:S(2)}) collective-permute-start(f32[1,23040]{1,0:T(1,128)} %get-tuple-element.75), channel_id=1, source_target_pairs={{2,0},{3,1},{6,4},{7,5},{10,8},{11,9},{14,12},{15,13},{18,16},{19,... | collective-permute-start | bytes 276488 | tf_op jit(solution)/shard_map/cond/branch_0_fun/ppermute | solution.py:491
  122.2 3.0 %collective-permute-start = (f32[1,23040]{1,0:T(1,128)}, f32[1,23040]{1,0:T(1,128)}, u32[]{:S(2)}, u32[]{:S(2)}) collective-permute-start(f32[1,23040]{1,0:T(1,128)} %get-tuple-element.75), channel_id=1, source_target_pairs={{1,0},{2,1},{3,2},{5,4},{6,5},{7,6},{9,8},{10,9},{11,10},{13,12},{... | collective-permute-start | bytes 276488 | tf_op jit(solution)/shard_map/cond/branch_0_fun/ppermute | solution.py:491
  125.3 8.2 %remap_tracers.3 = f32[9,4,23040]{2,1,0:T(4,128)} custom-call(f32[6,2,23040]{2,1,0:T(2,128)} %get-tuple-element.62.refs_0_, f32[6,2,23040]{2,1,0:T(2,128)} %get-tuple-element.63.refs_1_, f32[6,2,23040]{2,1,0:T(2,128)} %get-tuple-element.64.refs_2_, f32[6,2,23040]{2,1,0:T(2,128)} %get-tuple-element.65.refs_3_, f32[4,2,23040]{2,1,0:T(2,128)} %get-tuple-element.66.refs_4_, ...), custom_call_target="tpu_custom_call" | custom-call | flops 1000 | bytes 1000 | tf_op jit(solution)/shard_map/cond/branch_0_fun/remap_tracers/pallas_call | solution.py:410
  (41 shorter events, 10.7 us)
Async XLA Ops:
  7.2 97.6 %all-gather.4.cloned.1.call-start = ((), (), s32[]{:S(2)}) async-start(), calls=%async_computation | async-start | bytes 1843200 | tf_op jit(solution)/shard_map/all_gather | solution.py:472
  8.3 10.0 %copy-start = (f32[9,4,23040]{2,1,0:T(4,128)S(1)}, f32[9,4,23040]{2,1,0:T(4,128)}, u32[]{:S(2)}) copy-start(f32[9,4,23040]{2,1,0:T(4,128)} %refs_2_.3) | copy-start | bytes 9953284
  9.7 8.6 %copy-start.4 = (f32[4,23040]{1,0:T(4,128)S(1)}, f32[4,23040]{1,0:T(4,128)}, u32[]{:S(2)}) copy-start(f32[4,23040]{1,0:T(4,128)} %refs_0_.1) | copy-start | bytes 1105924
  10.6 17.4 %collective-permute-start.25 = (f32[3,4,11520]{2,1,0:T(4,128)}, f32[3,4,11520]{2,1,0:T(4,128)}, u32[]{:S(2)}, u32[]{:S(2)}) collective-permute-start(f32[3,4,11520]{2,1,0:T(4,128)} %pad_maximum_fusion.2), channel_id=1, source_target_pairs={{0,4},{4,8},{8,12},{12,16},{16,20},{20,24},{24,28},{28,32},{32,36}... | collective-permute-start | bytes 1658888 | tf_op jit(solution)/shard_map/ppermute | solution.py:460
  16.3 16.5 %collective-permute-start.26 = (f32[3,4,11520]{2,1,0:T(4,128)}, f32[3,4,11520]{2,1,0:T(4,128)}, u32[]{:S(2)}, u32[]{:S(2)}) collective-permute-start(f32[3,4,11520]{2,1,0:T(4,128)} %pad_maximum_fusion.3), channel_id=1, source_target_pairs={{4,0},{8,4},{12,8},{16,12},{20,16},{24,20},{28,24},{32,28},{36,32}... | collective-permute-start | bytes 1658888 | tf_op jit(solution)/shard_map/ppermute | solution.py:460
  19.7 32.5 %collective-permute-start.27 = (f32[6,4,11520]{2,1,0:T(4,128)}, f32[6,4,11520]{2,1,0:T(4,128)}, u32[]{:S(2)}, u32[]{:S(2)}) collective-permute-start(f32[6,4,11520]{2,1,0:T(4,128)} %pad_maximum_fusion), channel_id=1, source_target_pairs={{0,4},{4,8},{8,12},{12,16},{16,20},{20,24},{24,28},{28,32},{32,36}... | collective-permute-start | bytes 3317768 | tf_op jit(solution)/shard_map/ppermute | solution.py:460
  25.5 31.0 %collective-permute-start.28 = (f32[6,4,11520]{2,1,0:T(4,128)}, f32[6,4,11520]{2,1,0:T(4,128)}, u32[]{:S(2)}, u32[]{:S(2)}) collective-permute-start(f32[6,4,11520]{2,1,0:T(4,128)} %pad_maximum_fusion.1), channel_id=1, source_target_pairs={{4,0},{8,4},{12,8},{16,12},{20,16},{24,20},{28,24},{32,28},{36,32}... | collective-permute-start | bytes 3317768 | tf_op jit(solution)/shard_map/ppermute | solution.py:460
  45.7 37.6 %collective-permute-start.32 = (f32[4,4,11520]{2,1,0:T(4,128)}, f32[4,4,11520]{2,1,0:T(4,128)S(1)}, u32[]{:S(2)}, u32[]{:S(2)}) collective-permute-start(f32[4,4,11520]{2,1,0:T(4,128)} %get-tuple-element.141), channel_id=1, source_target_pairs={{4,0},{8,4},{12,8},{16,12},{20,16},{24,20},{28,24},{32,28},{36,32}... | collective-permute-start | bytes 2211848 | tf_op jit(solution)/shard_map/ppermute | solution.py:460
  47.6 35.7 %collective-permute-start.31 = (f32[4,4,11520]{2,1,0:T(4,128)}, f32[4,4,11520]{2,1,0:T(4,128)S(1)}, u32[]{:S(2)}, u32[]{:S(2)}) collective-permute-start(f32[4,4,11520]{2,1,0:T(4,128)} %get-tuple-element.142), channel_id=1, source_target_pairs={{0,4},{4,8},{8,12},{12,16},{16,20},{20,24},{24,28},{28,32},{32,36}... | collective-permute-start | bytes 2211848 | tf_op jit(solution)/shard_map/ppermute | solution.py:460
  75.9 36.4 %collective-permute-start.30 = (f32[6,2,23040]{2,1,0:T(2,128)}, f32[6,2,23040]{2,1,0:T(2,128)}, u32[]{:S(2)}, u32[]{:S(2)}) collective-permute-start(f32[6,2,23040]{2,1,0:T(2,128)} %get-tuple-element.131), channel_id=1, source_target_pairs={{1,0},{2,1},{3,2},{5,4},{6,5},{7,6},{9,8},{10,9},{11,10},{13,12},{... | collective-permute-start | bytes 3317768 | tf_op jit(solution)/shard_map/ppermute | solution.py:477
  81.9 22.1 %copy-start.13 = (f32[23040]{0:T(1024)S(1)}, f32[23040]{0:T(1024)}, u32[]{:S(2)}) copy-start(f32[23040]{0:T(1024)} %param.15) | copy-start | bytes 276484
  81.9 22.8 %copy-start.14 = (f32[16]{0:T(128)S(1)}, f32[16]{0:T(128)}, u32[]{:S(2)}) copy-start(f32[16]{0:T(128)} %weight_ref.1) | copy-start | bytes 196
  81.9 30.4 %collective-permute-start.29 = (f32[6,2,23040]{2,1,0:T(2,128)}, f32[6,2,23040]{2,1,0:T(2,128)}, u32[]{:S(2)}, u32[]{:S(2)}) collective-permute-start(f32[6,2,23040]{2,1,0:T(2,128)} %get-tuple-element.132), channel_id=1, source_target_pairs={{0,1},{1,2},{2,3},{4,5},{5,6},{6,7},{8,9},{9,10},{10,11},{12,13},{... | collective-permute-start | bytes 3317768 | tf_op jit(solution)/shard_map/ppermute | solution.py:477
  83.4 0.9 copy-start.6
  84.3 0.9 copy-start.7
  98.8 13.5 %collective-permute-start.34 = (f32[4,2,23040]{2,1,0:T(2,128)}, f32[4,2,23040]{2,1,0:T(2,128)}, u32[]{:S(2)}, u32[]{:S(2)}) collective-permute-start(f32[4,2,23040]{2,1,0:T(2,128)} %get-tuple-element.133), channel_id=1, source_target_pairs={{1,0},{2,1},{3,2},{5,4},{6,5},{7,6},{9,8},{10,9},{11,10},{13,12},{... | collective-permute-start | bytes 2211848 | tf_op jit(solution)/shard_map/ppermute | solution.py:477
  102.8 9.5 %collective-permute-start.33 = (f32[4,2,23040]{2,1,0:T(2,128)}, f32[4,2,23040]{2,1,0:T(2,128)}, u32[]{:S(2)}, u32[]{:S(2)}) collective-permute-start(f32[4,2,23040]{2,1,0:T(2,128)} %get-tuple-element.134), channel_id=1, source_target_pairs={{0,1},{1,2},{2,3},{4,5},{5,6},{6,7},{8,9},{9,10},{10,11},{12,13},{... | collective-permute-start | bytes 2211848 | tf_op jit(solution)/shard_map/ppermute | solution.py:477
  116.6 16.9 %collective-permute-start.2 = (f32[1,23040]{1,0:T(1,128)}, f32[1,23040]{1,0:T(1,128)}, u32[]{:S(2)}, u32[]{:S(2)}) collective-permute-start(f32[1,23040]{1,0:T(1,128)} %get-tuple-element.75), channel_id=1, source_target_pairs={{3,0},{7,4},{11,8},{15,12},{19,16},{23,20},{27,24},{31,28},{35,32}... | collective-permute-start | bytes 276488 | tf_op jit(solution)/shard_map/cond/branch_0_fun/ppermute | solution.py:491
  120.3 13.2 %collective-permute-start.1 = (f32[1,23040]{1,0:T(1,128)}, f32[1,23040]{1,0:T(1,128)}, u32[]{:S(2)}, u32[]{:S(2)}) collective-permute-start(f32[1,23040]{1,0:T(1,128)} %get-tuple-element.75), channel_id=1, source_target_pairs={{2,0},{3,1},{6,4},{7,5},{10,8},{11,9},{14,12},{15,13},{18,16},{19,... | collective-permute-start | bytes 276488 | tf_op jit(solution)/shard_map/cond/branch_0_fun/ppermute | solution.py:491
  122.2 11.3 %collective-permute-start = (f32[1,23040]{1,0:T(1,128)}, f32[1,23040]{1,0:T(1,128)}, u32[]{:S(2)}, u32[]{:S(2)}) collective-permute-start(f32[1,23040]{1,0:T(1,128)} %get-tuple-element.75), channel_id=1, source_target_pairs={{1,0},{2,1},{3,2},{5,4},{6,5},{7,6},{9,8},{10,9},{11,10},{13,12},{... | collective-permute-start | bytes 276488 | tf_op jit(solution)/shard_map/cond/branch_0_fun/ppermute | solution.py:491
  125.3 9.6 %copy-start.11 = (f32[4,23040]{1,0:T(4,128)S(1)}, f32[4,23040]{1,0:T(4,128)}, u32[]{:S(2)}) copy-start(f32[4,23040]{1,0:T(4,128)} %get-tuple-element.74) | copy-start | bytes 1105924 | tf_op jit(solution)/shard_map/cond
  135.2 0.7 copy-start.12
Sparse Core Ops, SparseCore 0:
  44.7 27.9 all-gather.3
where the time goes:
time: 144 us; the launch traced here: 143 us
  Pallas kernels  64.1 us (45%)
  starting transfers between devices  41 us (28%)
  between operations  14.9 us (10%)
  waiting for transfers between devices  9.11 us (6%)
  local copies, waits for them, and re-layouts  7 us (5%)
  other arithmetic  6.38 us (4%)
    pallas_call x2, Pallas kernels, transport(): pl.pallas_call(functools.partial(transport_kernel, bool(lead)), grid=(pai...  33.1 us
    ppermute x3, starting transfers between devices, beside(): lax.ppermute(last, 'lat', to_south)  13.9 us
    pallas_call x2, Pallas kernels, columnwise(): pl.pallas_call(kernel, grid=(cells // BLOCK,), out_shape=[jax.ShapeDtypeS...  12.5 us
    pallas_call x1, Pallas kernels, prepare(): pl.pallas_call(functools.partial(prepare_kernel, lat_total), grid=(1,), o...  11.7 us
    ppermute x2, starting transfers between devices, window(): lax.ppermute(first, 'lev', down(1))  9.97 us
    ppermute x3, waiting for transfers between devices, beside(): lax.ppermute(leading, 'lat', to_north)  9.07 us
    ppermute x3, starting transfers between devices, finish(): lax.ppermute(total, 'lev', down(by))  8.64 us
    pallas_call x1, Pallas kernels, edges(): pl.pallas_call(functools.partial(edges_kernel, rows), grid=(cells // BLOC...  6.87 us
  transfers between devices with their start and end apart: 14, of which 2 were waited for; matrix products, arithmetic and copies ran while one was open for 4% of the time, Pallas kernels for 42%

commit v1 on v0

--- a/solution.py
+++ b/solution.py
@@ -12,7 +12,7 @@
 HALF = 4
 ROWS = 8
 LAYERS = 4
-BLOCK = 3840
+BLOCK = 5760
 TOP = 1.0
 ROW_UNROLL = 4
 SMOOTH_UNROLL = 4
@@ -121,7 +121,7 @@
 
 def prepare_kernel(
     lat_total, row_ref, k_ref, delp_ref, wx_ref, wy_ref, north_ref, south_ref,
-    thick_ref, a_ref, b_ref, c_ref, d_ref, r_ref, x_ref, f1_ref, f2_ref,
+    thick_ref, *refs,
 ):
     def load(ref, field, put):
         widen(
@@ -131,6 +131,12 @@
             put,
         )
 
+    outs = refs[:5]
+    a_ref, b_ref, c_ref, d_ref, r_ref, x_ref, f1_ref, f2_ref, sem = refs[5:]
+    held = (a_ref, b_ref, c_ref, d_ref, r_ref)
+    copies = [
+        pltpu.make_async_copy(held[i], outs[i], sem.at[i]) for i in range(len(outs))
+    ]
     first = row_ref[0]
 
     def put_x(r, x):
@@ -148,6 +154,7 @@
         return carry
 
     lax.fori_loop(0, 13, face, 0)
+    copies[0].start()
     load(wx_ref, 1, put_x)
 
     def east(i, carry):
@@ -157,7 +164,10 @@
         return carry
 
     lax.fori_loop(0, 12, east, 0, unroll=2)
+    copies[1].start()
+    copies[2].start()
     load(delp_ref, 0, put_d)
+    copies[3].start()
     advance(d_ref, a_ref, b_ref, c_ref, f1_ref, 12, 0)
     advance(f1_ref, a_ref, b_ref, c_ref, f2_ref, 8, 2)
     smooth(f2_ref, k_ref)
@@ -165,17 +175,42 @@
     def store(base, x):
         thick_ref[:, pl.ds(base, x.shape[1])] = x[:LAYERS]
 
-    emit(f2_ref, store)
-
     def invert(i, carry):
         r_ref[i] = 1.0 / f2_ref[i]
         return carry
 
     lax.fori_loop(0, ROWS, invert, 0)
+    copies[4].start()
+    emit(f2_ref, store)
+    for copy in copies:
+        copy.wait()
 
 
 def whole(*shape):
     return pl.BlockSpec(shape, lambda *_: (0,) * len(shape))
+
+
+def pack_kernel(*refs):
+    north_ref, south_ref = refs[-2:]
+    half = north_ref.shape[2]
+    for i, ref in enumerate(refs[:-2]):
+        north_ref[i] = ref[:, :half]
+        south_ref[i] = ref[:, half:]
+
+
+def pack(*fields):
+    layers, cells = fields[0].shape
+    shape = (len(fields), layers, cells // 2)
+    return pl.pallas_call(
+        pack_kernel,
+        grid=(1,),
+        out_shape=[jax.ShapeDtypeStruct(shape, jnp.float32)] * 2,
+        in_specs=[whole(layers, cells)] * len(fields),
+        out_specs=[whole(*shape)] * 2,
+        compiler_params=params(),
+        cost_estimate=SMALL,
+        name="pack",
+    )(*fields)
 
 
 def prepare(first_row, k, delp, wx, wy, north, south, lat_total):
@@ -189,10 +224,11 @@
         out_shape=[jax.ShapeDtypeStruct(delp.shape, jnp.float32)]
         + [jax.ShapeDtypeStruct((n, 8, WIDE), jnp.float32) for n in rows],
         in_specs=[smem, smem, flat, flat, flat, halo, halo],
-        out_specs=[flat] + [whole(n, 8, WIDE) for n in rows],
+        out_specs=[flat] + [pl.BlockSpec(memory_space=pl.ANY)] * len(rows),
         scratch_shapes=[
-            pltpu.VMEM((n, 8, WIDE), jnp.float32) for n in (16, 12, 8)
-        ],
+            pltpu.VMEM((n, 8, WIDE), jnp.float32) for n in (*rows, 16, 12, 8)
+        ]
+        + [pltpu.SemaphoreType.DMA((len(rows),))],
         compiler_params=params(),
         cost_estimate=SMALL,
         name="prepare",
@@ -204,9 +240,20 @@
         theta_ref, *refs = refs
     (
         k_ref, lower_ref, upper_ref, north_ref, south_ref,
-        a_ref, b_ref, c_ref, d_ref, r_ref, first_ref, last_ref, f0_ref, f1_ref, f2_ref,
+        *sources, first_ref, last_ref, f0_ref, f1_ref, f2_ref,
+        a_ref, b_ref, c_ref, d_ref, r_ref, sem,
     ) = refs
     pair = pl.program_id(0)
+    held = (a_ref, b_ref, c_ref, d_ref, r_ref)
+    copies = [
+        pltpu.make_async_copy(sources[i], held[i], sem.at[i]) for i in range(len(held))
+    ]
+
+    @pl.when(pair == 0)
+    def _():
+        for i in (3, 0, 1, 2, 4):
+            copies[i].start()
+        copies[3].wait()
 
     def lower(s):
         x = lower_ref[0, :, pl.ds(s, WIDE)]
@@ -227,6 +274,12 @@
         ),
         put,
     )
+
+    @pl.when(pair == 0)
+    def _():
+        for i in (0, 1, 2, 4):
+            copies[i].wait()
+
     advance(f0_ref, a_ref, b_ref, c_ref, f1_ref, 12, 0)
     advance(f1_ref, a_ref, b_ref, c_ref, f2_ref, 8, 2)
     smooth(f2_ref, k_ref)
@@ -249,7 +302,7 @@
         pl.BlockSpec(memory_space=pltpu.SMEM),
         field(lambda p: (jnp.maximum(first + 2 * p - lead, first), 0, 0)),
         field(lambda p: (first + 2 * p + 1 - lead, 0, 0)),
-        halo, halo, *[whole(*x.shape) for x in rows],
+        halo, halo, *[pl.BlockSpec(memory_space=pl.ANY)] * len(rows),
     ]
     args = [k, tracers, tracers, north, south, *rows]
     half = pl.BlockSpec((2, 2, cells), lambda p: (p, 0, 0))
@@ -263,8 +316,10 @@
         in_specs=in_specs,
         out_specs=[half, half],
         scratch_shapes=[
-            pltpu.VMEM((n, 8, WIDE), jnp.float32) for n in (16, 12, 8)
-        ],
+            pltpu.VMEM((n, 8, WIDE), jnp.float32)
+            for n in (16, 12, 8, *[x.shape[0] for x in rows])
+        ]
+        + [pltpu.SemaphoreType.DMA((len(rows),))],
         compiler_params=params(),
         cost_estimate=SMALL,
         name="transport",
@@ -457,13 +512,16 @@
     def beside(parts):
         last = jnp.concatenate([p[:, :, half:] for p in parts], axis=0)
         leading = jnp.concatenate([p[:, :, :half] for p in parts], axis=0)
+        return exchange(leading, last)
+
+    def exchange(leading, last):
         return lax.ppermute(last, "lat", to_south), lax.ppermute(leading, "lat", to_north)
 
     first_row = (band * ROWS).astype(jnp.int32)
     row_index = (first_row + jnp.arange(ROWS, dtype=jnp.int32)).astype(jnp.float32)
     latitude = jnp.pi * ((row_index + 0.5) / lat_total - 0.5)
     k = 0.25 * jnp.maximum(0.0, 1.0 - 2.0 * jnp.cos(latitude))
-    north, south = beside([delp[None], wind_x[None], wind_y[None]])
+    north, south = exchange(*pack(delp, wind_x, wind_y))
     halo_one = beside([theta[None], tracers[SPLIT:]])
     halo_two = beside([tracers[:SPLIT]])
     thick, *rows = prepare(

time: 144 us -> 140 us (0.972)
  other arithmetic: 6.38 us -> 3.41 us
    pallas_call x0 -> x1, Pallas kernels: none -> 2.32 us  [pack(): pl.pallas_call(pack_kernel, grid=(1,), out_shape=[jax.ShapeDtypeStruct(sh...]
    concatenate x2 -> x1, other arithmetic: 2.26 us -> 0.24 us  [beside(): last = jnp.concatenate([p[:, :, half:] for p in parts], axis=0)]
    pallas_call x2, Pallas kernels: 12.5 us -> 11 us  [columnwise(): pl.pallas_call(kernel, grid=(cells // BLOCK,), out_shape=[jax.ShapeDtypeS...]
    slice x5 -> x3, local copies, waits for them, and re-layouts: 3.77 us -> 4.18 us  [beside(): leading = jnp.concatenate([p[:, :, :half] for p in parts], axis=0)]
  transfers between devices with their start and end apart: 14 -> 14, of which waited for: 2 -> 2; matrix products, arithmetic and copies ran while one was open for 4% -> 5% of each run, Pallas kernels for 42% -> 42%
where the time goes in v1:
time: 140 us; the launch traced here: 139 us
  Pallas kernels  64.2 us (46%)
  starting transfers between devices  41 us (29%)
  between operations  14.9 us (11%)
  waiting for transfers between devices  8.43 us (6%)
  local copies, waits for them, and re-layouts  6.62 us (5%)
  other arithmetic  3.41 us (2%)
    pallas_call x2, Pallas kernels, transport(): pl.pallas_call(functools.partial(transport_kernel, bool(lead)), grid=(pai...  33.3 us
    ppermute x3, starting transfers between devices, exchange(): lax.ppermute(last, 'lat', to_south)  13.9 us
    pallas_call x2, Pallas kernels, columnwise(): pl.pallas_call(kernel, grid=(cells // BLOCK,), out_shape=[jax.ShapeDtypeS...  11 us
    pallas_call x1, Pallas kernels, prepare(): pl.pallas_call(functools.partial(prepare_kernel, lat_total), grid=(1,), o...  10.5 us
    ppermute x2, starting transfers between devices, window(): lax.ppermute(first, 'lev', down(1))  10.2 us
    ppermute x3, starting transfers between devices, finish(): lax.ppermute(total, 'lev', down(by))  8.46 us
    ppermute x3, waiting for transfers between devices, exchange(): lax.ppermute(leading, 'lat', to_north)  8.39 us
    pallas_call x1, Pallas kernels, edges(): pl.pallas_call(functools.partial(edges_kernel, rows), grid=(cells // BLOC...  7.03 us
  transfers between devices with their start and end apart: 14, of which 2 were waited for; matrix products, arithmetic and copies ran while one was open for 5% of the time, Pallas kernels for 42%

profile of v1, /device:TPU:99, one launch (start us, length us, event | category | flops | bytes accessed | tf_op | source)
XLA Modules:
  0.0 139.0 jit_solution(9355906252821813228)
XLA Ops:
  7.2 2.3 %pack.1 = (f32[3,4,11520]{2,1,0:T(4,128)}, f32[3,4,11520]{2,1,0:T(4,128)}) custom-call(f32[4,23040]{1,0:T(4,128)} %delp_ref.1, f32[4,23040]{1,0:T(4,128)} %wx_ref.1, f32[4,23040]{1,0:T(4,128)} %wy_ref.1), custom_call_target="tpu_custom_call" | custom-call | flops 1000 | bytes 1000 | tf_op jit(solution)/shard_map/pack/pallas_call | solution.py:204
  9.5 4.7 %collective-permute-start.25 = (f32[3,4,11520]{2,1,0:T(4,128)}, f32[3,4,11520]{2,1,0:T(4,128)}, u32[]{:S(2)}, u32[]{:S(2)}) collective-permute-start(f32[3,4,11520]{2,1,0:T(4,128)} %get-tuple-element.126), channel_id=1, source_target_pairs={{0,4},{4,8},{8,12},{12,16},{16,20},{20,24},{24,28},{28,32},{32,36}... | collective-permute-start | bytes 1658888 | tf_op jit(solution)/shard_map/ppermute | solution.py:518
  14.3 1.9 %collective-permute-start.26 = (f32[3,4,11520]{2,1,0:T(4,128)}, f32[3,4,11520]{2,1,0:T(4,128)}, u32[]{:S(2)}, u32[]{:S(2)}) collective-permute-start(f32[3,4,11520]{2,1,0:T(4,128)} %get-tuple-element.127), channel_id=1, source_target_pairs={{4,0},{8,4},{12,8},{16,12},{20,16},{24,20},{28,24},{32,28},{36,32}... | collective-permute-start | bytes 1658888 | tf_op jit(solution)/shard_map/ppermute | solution.py:518
  16.3 1.6 %fusion.1 = (f32[5,4,11520]{2,1,0:T(4,128)S(1)}, f32[5,4,11520]{2,1,0:T(4,128)S(1)}) fusion(f32[9,4,23040]{2,1,0:T(4,128)} %refs_2_.5), kind=kLoop, calls=%fused_computation.10 | loop fusion | bytes 3686400 | tf_op jit(solution)/shard_map/slice | solution.py:514
  18.1 4.6 %collective-permute-start.27 = (f32[6,4,11520]{2,1,0:T(4,128)S(1)}, f32[6,4,11520]{2,1,0:T(4,128)S(1)}, u32[]{:S(2)}, u32[]{:S(2)}) collective-permute-start(f32[6,4,11520]{2,1,0:T(4,128)S(1)} %pad_maximum_fusion), channel_id=1, source_target_pairs={{0,4},{4,8},{8,12},{12,16},{16,20},{20,24},{24,28},{28,32},{32,36}... | collective-permute-start | bytes 3317768 | tf_op jit(solution)/shard_map/ppermute | solution.py:518
  23.9 1.9 %collective-permute-start.28 = (f32[6,4,11520]{2,1,0:T(4,128)}, f32[6,4,11520]{2,1,0:T(4,128)S(1)}, u32[]{:S(2)}, u32[]{:S(2)}) collective-permute-start(f32[6,4,11520]{2,1,0:T(4,128)} %pad_maximum_fusion.1), channel_id=1, source_target_pairs={{4,0},{8,4},{12,8},{16,12},{20,16},{24,20},{28,24},{32,28},{36,32}... | collective-permute-start | bytes 3317768 | tf_op jit(solution)/shard_map/ppermute | solution.py:518
  26.4 4.4 %collective-permute-done.26.south_ref = f32[3,4,11520]{2,1,0:T(4,128)} collective-permute-done((f32[3,4,11520]{2,1,0:T(4,128)}, f32[3,4,11520]{2,1,0:T(4,128)}, u32[]{:S(2)}, u32[]{:S(2)}) %collective-permute-start.26) | collective-permute-done | bytes 552992 | tf_op jit(solution)/shard_map/ppermute | solution.py:518
  30.8 10.5 %prepare.1 = (f32[4,23040]{1,0:T(4,128)}, f32[13,8,2944]{2,1,0:T(8,128)}, f32[12,8,2944]{2,1,0:T(8,128)}, f32[12,8,2944]{2,1,0:T(8,128)}, f32[16,8,2944]{2,1,0:T(8,128)}, /*index=5*/f32[8,8,2944]{2,1,0:T(8,128)}) custom-call(s32[1]{0:T(128)} %bitcast.2.row_ref, f32[8]{0:T(128)} %maximum_multiply_fusion.k_ref.refs_1_.refs_0_, f32[4,23040]{1,0:T(4,128)} %delp_ref.1, ...), custom_call_target="tpu_custom_call" | custom-call | flops 1000 | bytes 1000 | tf_op jit(solution)/shard_map/prepare/pallas_call | solution.py:221
  41.3 2.6 %fusion = (f32[4,4,11520]{2,1,0:T(4,128)}, f32[4,4,11520]{2,1,0:T(4,128)}) fusion(f32[9,4,23040]{2,1,0:T(4,128)} %refs_2_.5), kind=kLoop, calls=%fused_computation.9 | loop fusion | bytes 2949120 | tf_op jit(solution)/shard_map/slice | solution.py:514
  43.9 1.9 %collective-permute-start.32 = (f32[4,4,11520]{2,1,0:T(4,128)}, f32[4,4,11520]{2,1,0:T(4,128)}, u32[]{:S(2)}, u32[]{:S(2)}) collective-permute-start(f32[4,4,11520]{2,1,0:T(4,128)} %get-tuple-element.145), channel_id=1, source_target_pairs={{4,0},{8,4},{12,8},{16,12},{20,16},{24,20},{28,24},{32,28},{36,32}... | collective-permute-start | bytes 2211848 | tf_op jit(solution)/shard_map/ppermute | solution.py:518
  45.8 4.6 %collective-permute-start.31 = (f32[4,4,11520]{2,1,0:T(4,128)}, f32[4,4,11520]{2,1,0:T(4,128)}, u32[]{:S(2)}, u32[]{:S(2)}) collective-permute-start(f32[4,4,11520]{2,1,0:T(4,128)} %get-tuple-element.146), channel_id=1, source_target_pairs={{0,4},{4,8},{8,12},{12,16},{16,20},{20,24},{24,28},{28,32},{32,36}... | collective-permute-start | bytes 2211848 | tf_op jit(solution)/shard_map/ppermute | solution.py:518
  50.4 4.0 %collective-permute-done.28.refs_5_ = f32[6,4,11520]{2,1,0:T(4,128)S(1)} collective-permute-done((f32[6,4,11520]{2,1,0:T(4,128)}, f32[6,4,11520]{2,1,0:T(4,128)S(1)}, u32[]{:S(2)}, u32[]{:S(2)}) %collective-permute-start.28) | collective-permute-done | bytes 1105952 | tf_op jit(solution)/shard_map/ppermute | solution.py:518
  55.4 19.2 %transport.2 = (f32[6,2,23040]{2,1,0:T(2,128)}, f32[6,2,23040]{2,1,0:T(2,128)}) custom-call(f32[4,23040]{1,0:T(4,128)} %refs_0_.3, f32[8]{0:T(128)} %maximum_multiply_fusion.k_ref.refs_1_.refs_0_, f32[9,4,23040]{2,1,0:T(4,128)} %refs_2_.5, f32[9,4,23040]{2,1,0:T(4,128)} %refs_2_.5, f32[6,4,11520]{2,1,0:T(4,128)} %copy-done.5, f32[6,4,11520]{2,1,0:T(4,128)} %copy-done.6, ...), custom_call_target="tpu_custom_call" | custom-call | flops 1000 | bytes 1000 | tf_op jit(solution)/shard_map/transport/pallas_call | solution.py:312
  74.6 6.2 %collective-permute-start.30 = (f32[6,2,23040]{2,1,0:T(2,128)}, f32[6,2,23040]{2,1,0:T(2,128)}, u32[]{:S(2)}, u32[]{:S(2)}) collective-permute-start(f32[6,2,23040]{2,1,0:T(2,128)} %get-tuple-element.135), channel_id=1, source_target_pairs={{1,0},{2,1},{3,2},{5,4},{6,5},{7,6},{9,8},{10,9},{11,10},{13,12},{... | collective-permute-start | bytes 3317768 | tf_op jit(solution)/shard_map/ppermute | solution.py:535
  80.9 1.4 %collective-permute-start.29 = (f32[6,2,23040]{2,1,0:T(2,128)}, f32[6,2,23040]{2,1,0:T(2,128)}, u32[]{:S(2)}, u32[]{:S(2)}) collective-permute-start(f32[6,2,23040]{2,1,0:T(2,128)} %get-tuple-element.136), channel_id=1, source_target_pairs={{0,1},{1,2},{2,3},{4,5},{5,6},{6,7},{8,9},{9,10},{10,11},{12,13},{... | collective-permute-start | bytes 3317768 | tf_op jit(solution)/shard_map/ppermute | solution.py:535
  82.3 14.0 %transport.3 = (f32[4,2,23040]{2,1,0:T(2,128)}, f32[4,2,23040]{2,1,0:T(2,128)}) custom-call(f32[8]{0:T(128)} %maximum_multiply_fusion.k_ref.refs_1_.refs_0_, f32[9,4,23040]{2,1,0:T(4,128)} %refs_2_.5, f32[9,4,23040]{2,1,0:T(4,128)} %refs_2_.5, f32[4,4,11520]{2,1,0:T(4,128)} %collective-permute-done.31.refs_3_, ...), custom_call_target="tpu_custom_call" | custom-call | flops 1000 | bytes 1000 | tf_op jit(solution)/shard_map/transport/pallas_call | solution.py:312
  96.4 3.9 %collective-permute-start.34 = (f32[4,2,23040]{2,1,0:T(2,128)}, f32[4,2,23040]{2,1,0:T(2,128)}, u32[]{:S(2)}, u32[]{:S(2)}) collective-permute-start(f32[4,2,23040]{2,1,0:T(2,128)} %get-tuple-element.137), channel_id=1, source_target_pairs={{1,0},{2,1},{3,2},{5,4},{6,5},{7,6},{9,8},{10,9},{11,10},{13,12},{... | collective-permute-start | bytes 2211848 | tf_op jit(solution)/shard_map/ppermute | solution.py:535
  102.3 7.0 %edges.3 = (f32[10,4,23040]{2,1,0:T(4,128)S(1)}, f32[4,23040]{1,0:T(4,128)}, f32[4,23040]{1,0:T(4,128)S(1)}, s32[1]{0:T(128)}) custom-call(f32[16]{0:T(128)S(1)} %copy-done.13, s32[1]{0:T(128)} %bitcast.1.lev_ref, f32[4,4,23040]{2,1,0:T(4,128)} %all-gather.4.cloned.1.call-done.thick_ref), custom_call_target="tpu_custom_call" | custom-call | flops 1000 | bytes 1000 | tf_op jit(solution)/shard_map/edges/pallas_call | solution.py:403
  110.1 21.4 %conditional.1 = (f32[9,4,23040]{2,1,0:T(4,128)}, f32[4,23040]{1,0:T(4,128)}, f32[4,23040]{1,0:T(4,128)S(1)}) conditional(s32[]{:T(128)} %bitcast.4, (f32[6,2,23040]{2,1,0:T(2,128)}, f32[6,2,23040]{2,1,0:T(2,128)}, f32[6,2,23040]{2,1,0:T(2,128)}, f32[6,2,23040]{2,1,0:T(2,128)}, f32[4,2,23040]{2,1,0:T(2,128)}, ...), branch_computations={%region_0.0_spmd, %region_1.0_spmd, %region_2.0_spmd} | conditional | flops 141240 | bytes 64607952 | solution.py:581
  110.1 3.6 %remap_theta.3 = (f32[4,23040]{1,0:T(4,128)}, f32[4,23040]{1,0:T(4,128)}, f32[1,23040]{1,0:T(1,128)}) custom-call(f32[6,2,23040]{2,1,0:T(2,128)} %get-tuple-element.62.refs_0_, f32[6,2,23040]{2,1,0:T(2,128)} %get-tuple-element.63.refs_1_, f32[6,2,23040]{2,1,0:T(2,128)} %get-tuple-element.64.refs_2_, f32[6,2,23040]{2,1,0:T(2,128)} %get-tuple-element.65.refs_3_, ...), custom_call_target="tpu_custom_call" | custom-call | flops 1000 | bytes 1000 | tf_op jit(solution)/shard_map/cond/branch_0_fun/remap_theta/pallas_call | solution.py:465
  113.6 3.6 %collective-permute-start.2 = (f32[1,23040]{1,0:T(1,128)}, f32[1,23040]{1,0:T(1,128)}, u32[]{:S(2)}, u32[]{:S(2)}) collective-permute-start(f32[1,23040]{1,0:T(1,128)} %get-tuple-element.75), channel_id=1, source_target_pairs={{3,0},{7,4},{11,8},{15,12},{19,16},{23,20},{27,24},{31,28},{35,32}... | collective-permute-start | bytes 276488 | tf_op jit(solution)/shard_map/cond/branch_0_fun/ppermute | solution.py:549
  117.2 1.9 %collective-permute-start.1 = (f32[1,23040]{1,0:T(1,128)}, f32[1,23040]{1,0:T(1,128)}, u32[]{:S(2)}, u32[]{:S(2)}) collective-permute-start(f32[1,23040]{1,0:T(1,128)} %get-tuple-element.75), channel_id=1, source_target_pairs={{2,0},{3,1},{6,4},{7,5},{10,8},{11,9},{14,12},{15,13},{18,16},{19,... | collective-permute-start | bytes 276488 | tf_op jit(solution)/shard_map/cond/branch_0_fun/ppermute | solution.py:549
  119.2 2.9 %collective-permute-start = (f32[1,23040]{1,0:T(1,128)}, f32[1,23040]{1,0:T(1,128)}, u32[]{:S(2)}, u32[]{:S(2)}) collective-permute-start(f32[1,23040]{1,0:T(1,128)} %get-tuple-element.75), channel_id=1, source_target_pairs={{1,0},{2,1},{3,2},{5,4},{6,5},{7,6},{9,8},{10,9},{11,10},{13,12},{... | collective-permute-start | bytes 276488 | tf_op jit(solution)/shard_map/cond/branch_0_fun/ppermute | solution.py:549
  122.1 7.5 %remap_tracers.3 = f32[9,4,23040]{2,1,0:T(4,128)} custom-call(f32[6,2,23040]{2,1,0:T(2,128)} %get-tuple-element.62.refs_0_, f32[6,2,23040]{2,1,0:T(2,128)} %get-tuple-element.63.refs_1_, f32[6,2,23040]{2,1,0:T(2,128)} %get-tuple-element.64.refs_2_, f32[6,2,23040]{2,1,0:T(2,128)} %get-tuple-element.65.refs_3_, f32[4,2,23040]{2,1,0:T(2,128)} %get-tuple-element.66.refs_4_, ...), custom_call_target="tpu_custom_call" | custom-call | flops 1000 | bytes 1000 | tf_op jit(solution)/shard_map/cond/branch_0_fun/remap_tracers/pallas_call | solution.py:465
  (36 shorter events, 7.2 us)
Async XLA Ops:
  7.2 9.1 %copy-start.3 = (f32[4,23040]{1,0:T(4,128)S(1)}, f32[4,23040]{1,0:T(4,128)}, u32[]{:S(2)}) copy-start(f32[4,23040]{1,0:T(4,128)} %refs_0_.3) | copy-start | bytes 1105924
  7.2 95.1 %all-gather.4.cloned.1.call-start = ((), (), s32[]{:S(2)}) async-start(), calls=%async_computation | async-start | bytes 1843200 | tf_op jit(solution)/shard_map/all_gather | solution.py:530
  9.5 16.9 %collective-permute-start.25 = (f32[3,4,11520]{2,1,0:T(4,128)}, f32[3,4,11520]{2,1,0:T(4,128)}, u32[]{:S(2)}, u32[]{:S(2)}) collective-permute-start(f32[3,4,11520]{2,1,0:T(4,128)} %get-tuple-element.126), channel_id=1, source_target_pairs={{0,4},{4,8},{8,12},{12,16},{16,20},{20,24},{24,28},{28,32},{32,36}... | collective-permute-start | bytes 1658888 | tf_op jit(solution)/shard_map/ppermute | solution.py:518
  14.3 16.5 %collective-permute-start.26 = (f32[3,4,11520]{2,1,0:T(4,128)}, f32[3,4,11520]{2,1,0:T(4,128)}, u32[]{:S(2)}, u32[]{:S(2)}) collective-permute-start(f32[3,4,11520]{2,1,0:T(4,128)} %get-tuple-element.127), channel_id=1, source_target_pairs={{4,0},{8,4},{12,8},{16,12},{20,16},{24,20},{28,24},{32,28},{36,32}... | collective-permute-start | bytes 1658888 | tf_op jit(solution)/shard_map/ppermute | solution.py:518
  18.1 32.3 %collective-permute-start.27 = (f32[6,4,11520]{2,1,0:T(4,128)S(1)}, f32[6,4,11520]{2,1,0:T(4,128)S(1)}, u32[]{:S(2)}, u32[]{:S(2)}) collective-permute-start(f32[6,4,11520]{2,1,0:T(4,128)S(1)} %pad_maximum_fusion), channel_id=1, source_target_pairs={{0,4},{4,8},{8,12},{12,16},{16,20},{20,24},{24,28},{28,32},{32,36}... | collective-permute-start | bytes 3317768 | tf_op jit(solution)/shard_map/ppermute | solution.py:518
  23.9 30.5 %collective-permute-start.28 = (f32[6,4,11520]{2,1,0:T(4,128)}, f32[6,4,11520]{2,1,0:T(4,128)S(1)}, u32[]{:S(2)}, u32[]{:S(2)}) collective-permute-start(f32[6,4,11520]{2,1,0:T(4,128)} %pad_maximum_fusion.1), channel_id=1, source_target_pairs={{4,0},{8,4},{12,8},{16,12},{20,16},{24,20},{28,24},{32,28},{36,32}... | collective-permute-start | bytes 3317768 | tf_op jit(solution)/shard_map/ppermute | solution.py:518
  43.9 38.4 %collective-permute-start.32 = (f32[4,4,11520]{2,1,0:T(4,128)}, f32[4,4,11520]{2,1,0:T(4,128)}, u32[]{:S(2)}, u32[]{:S(2)}) collective-permute-start(f32[4,4,11520]{2,1,0:T(4,128)} %get-tuple-element.145), channel_id=1, source_target_pairs={{4,0},{8,4},{12,8},{16,12},{20,16},{24,20},{28,24},{32,28},{36,32}... | collective-permute-start | bytes 2211848 | tf_op jit(solution)/shard_map/ppermute | solution.py:518
  45.8 36.5 %collective-permute-start.31 = (f32[4,4,11520]{2,1,0:T(4,128)}, f32[4,4,11520]{2,1,0:T(4,128)}, u32[]{:S(2)}, u32[]{:S(2)}) collective-permute-start(f32[4,4,11520]{2,1,0:T(4,128)} %get-tuple-element.146), channel_id=1, source_target_pairs={{0,4},{4,8},{8,12},{12,16},{16,20},{20,24},{24,28},{28,32},{32,36}... | collective-permute-start | bytes 2211848 | tf_op jit(solution)/shard_map/ppermute | solution.py:518
  50.4 4.0 %copy-start.5 = (f32[6,4,11520]{2,1,0:T(4,128)}, f32[6,4,11520]{2,1,0:T(4,128)S(1)}, u32[]{:S(2)}) copy-start(f32[6,4,11520]{2,1,0:T(4,128)S(1)} %collective-permute-done.27.refs_4_) | copy-start | bytes 3317764
  54.4 1.0 copy-start.6
  74.6 35.4 %collective-permute-start.30 = (f32[6,2,23040]{2,1,0:T(2,128)}, f32[6,2,23040]{2,1,0:T(2,128)}, u32[]{:S(2)}, u32[]{:S(2)}) collective-permute-start(f32[6,2,23040]{2,1,0:T(2,128)} %get-tuple-element.135), channel_id=1, source_target_pairs={{1,0},{2,1},{3,2},{5,4},{6,5},{7,6},{9,8},{10,9},{11,10},{13,12},{... | collective-permute-start | bytes 3317768 | tf_op jit(solution)/shard_map/ppermute | solution.py:535
  80.9 20.7 %copy-start.12 = (f32[23040]{0:T(1024)S(1)}, f32[23040]{0:T(1024)}, u32[]{:S(2)}) copy-start(f32[23040]{0:T(1024)} %param.15) | copy-start | bytes 276484
  80.9 21.4 %copy-start.13 = (f32[16]{0:T(128)S(1)}, f32[16]{0:T(128)}, u32[]{:S(2)}) copy-start(f32[16]{0:T(128)} %weight_ref.1) | copy-start | bytes 196
  80.9 29.2 %collective-permute-start.29 = (f32[6,2,23040]{2,1,0:T(2,128)}, f32[6,2,23040]{2,1,0:T(2,128)}, u32[]{:S(2)}, u32[]{:S(2)}) collective-permute-start(f32[6,2,23040]{2,1,0:T(2,128)} %get-tuple-element.136), channel_id=1, source_target_pairs={{0,1},{1,2},{2,3},{4,5},{5,6},{6,7},{8,9},{9,10},{10,11},{12,13},{... | collective-permute-start | bytes 3317768 | tf_op jit(solution)/shard_map/ppermute | solution.py:535
  96.4 13.6 %collective-permute-start.34 = (f32[4,2,23040]{2,1,0:T(2,128)}, f32[4,2,23040]{2,1,0:T(2,128)}, u32[]{:S(2)}, u32[]{:S(2)}) collective-permute-start(f32[4,2,23040]{2,1,0:T(2,128)} %get-tuple-element.137), channel_id=1, source_target_pairs={{1,0},{2,1},{3,2},{5,4},{6,5},{7,6},{9,8},{10,9},{11,10},{13,12},{... | collective-permute-start | bytes 2211848 | tf_op jit(solution)/shard_map/ppermute | solution.py:535
  100.3 9.7 %collective-permute-start.33 = (f32[4,2,23040]{2,1,0:T(2,128)}, f32[4,2,23040]{2,1,0:T(2,128)}, u32[]{:S(2)}, u32[]{:S(2)}) collective-permute-start(f32[4,2,23040]{2,1,0:T(2,128)} %get-tuple-element.138), channel_id=1, source_target_pairs={{0,1},{1,2},{2,3},{4,5},{5,6},{6,7},{8,9},{9,10},{10,11},{12,13},{... | collective-permute-start | bytes 2211848 | tf_op jit(solution)/shard_map/ppermute | solution.py:535
  113.6 15.9 %collective-permute-start.2 = (f32[1,23040]{1,0:T(1,128)}, f32[1,23040]{1,0:T(1,128)}, u32[]{:S(2)}, u32[]{:S(2)}) collective-permute-start(f32[1,23040]{1,0:T(1,128)} %get-tuple-element.75), channel_id=1, source_target_pairs={{3,0},{7,4},{11,8},{15,12},{19,16},{23,20},{27,24},{31,28},{35,32}... | collective-permute-start | bytes 276488 | tf_op jit(solution)/shard_map/cond/branch_0_fun/ppermute | solution.py:549
  117.2 12.3 %collective-permute-start.1 = (f32[1,23040]{1,0:T(1,128)}, f32[1,23040]{1,0:T(1,128)}, u32[]{:S(2)}, u32[]{:S(2)}) collective-permute-start(f32[1,23040]{1,0:T(1,128)} %get-tuple-element.75), channel_id=1, source_target_pairs={{2,0},{3,1},{6,4},{7,5},{10,8},{11,9},{14,12},{15,13},{18,16},{19,... | collective-permute-start | bytes 276488 | tf_op jit(solution)/shard_map/cond/branch_0_fun/ppermute | solution.py:549
  119.2 10.4 %collective-permute-start = (f32[1,23040]{1,0:T(1,128)}, f32[1,23040]{1,0:T(1,128)}, u32[]{:S(2)}, u32[]{:S(2)}) collective-permute-start(f32[1,23040]{1,0:T(1,128)} %get-tuple-element.75), channel_id=1, source_target_pairs={{1,0},{2,1},{3,2},{5,4},{6,5},{7,6},{9,8},{10,9},{11,10},{13,12},{... | collective-permute-start | bytes 276488 | tf_op jit(solution)/shard_map/cond/branch_0_fun/ppermute | solution.py:549
  122.1 8.8 %copy-start.10 = (f32[4,23040]{1,0:T(4,128)S(1)}, f32[4,23040]{1,0:T(4,128)}, u32[]{:S(2)}) copy-start(f32[4,23040]{1,0:T(4,128)} %get-tuple-element.74) | copy-start | bytes 1105924 | tf_op jit(solution)/shard_map/cond
  131.4 0.7 copy-start.11
Sparse Core Ops, SparseCore 0:
  41.4 28.0 all-gather.3
